TPU v7x, 32 devices: a whole 2x2x4 slice. The times are simulated.
32 devices in a mesh: grp: 2 (over x), seq: 16 (over z, y, core).
Axes of the slice: x: 2, y: 2, z: 4, core: 2. Of those that a mesh axis runs over, the one named last changes fastest.
Arguments:
- tokens: bfloat16 [16384, 1024], P(('grp', 'seq')), may hold values from -20 to 20
- qkv_weight: bfloat16 [1024, 1536], replicated, may hold values from -2 to 2
- cov_embed: bfloat16 [64, 1024], P(('grp', 'seq')), may hold values from -20 to 20
- cov_slot: int32 [32], replicated, may hold values from 0 to 63, as said below
- block_links: int32 [128, 2], P(('grp', 'seq')), may hold values from 0 to 1, as said below
Outputs:
- attended: bfloat16 [16384, 512], P(('grp', 'seq'))
Inputs may be any that keep to these rules, and one draw needn't show every extreme that they name: The values are distinct; covariate c is held in slot cov_slot[c], on the device that holds that row of cov_embed. block_links[b, 1] equals block_links[b + 1, 0]; block_links[0, 0] and block_links[127, 1] are 0.
All inputs are finite; a program needn't handle non-finite values.
Results may differ from a plain program's by a relative error of at most 0.0015.
The roundings to bfloat16 on the way count: a program that leaves them out, or rounds other values in their place, can miss the bound.
Values may be sent and summed in bfloat16 or wider, within the bound.
A program may use at most 64 MiB of HBM per device.

v0:
```python
import math

import jax
import jax.numpy as jnp
from jax import lax
from jax.sharding import PartitionSpec as P

HEADS = 8
BLOCK = 128


masked_score = -1e30


def extended(cells, sides, width):
    for axis, dim in sides:
        count = lax.axis_size(axis)
        ends = count - 1
        head = lax.slice_in_dim(cells, 0, width, axis=dim)
        tail = lax.slice_in_dim(cells, cells.shape[dim] - width, cells.shape[dim], axis=dim)
        cells = jnp.concatenate(
            [
                lax.ppermute(tail, axis, [(i, (i + 1) % count) for i in range(ends)]),
                cells,
                lax.ppermute(head, axis, [((i + 1) % count, i) for i in range(ends)]),
            ],
            axis=dim,
        )
    return cells


def window_attend(queries, before, middle, after, left_open, right_open, cov_kv, head_count):
    blocks, block_rows, attn_width = queries.shape
    head_width = attn_width // head_count
    score_scale = 1.0 / math.sqrt(head_width)
    query_heads = queries.reshape(blocks, block_rows, head_count, head_width)

    def divide_parts(joined):
        key_part = joined[:, :, :attn_width].reshape(blocks, block_rows, head_count, head_width)
        value_part = joined[:, :, attn_width:].reshape(blocks, block_rows, head_count, head_width)
        return (key_part, value_part)

    key_before, value_before = divide_parts(before)
    key_middle, value_middle = divide_parts(middle)
    key_after, value_after = divide_parts(after)
    cov_count = cov_kv.shape[0]
    cov_keys = cov_kv[:, :attn_width].reshape(cov_count, head_count, head_width)
    cov_values = cov_kv[:, attn_width:].reshape(cov_count, head_count, head_width)

    def local_scores(key_part):
        return (
            jnp.einsum("nqhd,nkhd->nqhk", query_heads, key_part, preferred_element_type=jnp.float32)
            * score_scale
        )

    score_before = jnp.where(
        (left_open > 0)[:, None, None, None], local_scores(key_before), masked_score
    )
    score_middle = local_scores(key_middle)
    score_after = jnp.where(
        (right_open > 0)[:, None, None, None], local_scores(key_after), masked_score
    )
    score_global = (
        jnp.einsum("nqhd,chd->nqhc", query_heads, cov_keys, preferred_element_type=jnp.float32)
        * score_scale
    )
    highest = jnp.maximum(
        jnp.maximum(
            jnp.max(score_before, axis=-1, keepdims=True),
            jnp.max(score_middle, axis=-1, keepdims=True),
        ),
        jnp.maximum(
            jnp.max(score_after, axis=-1, keepdims=True),
            jnp.max(score_global, axis=-1, keepdims=True),
        ),
    )
    weight_before = jnp.exp(score_before - highest)
    weight_middle = jnp.exp(score_middle - highest)
    weight_after = jnp.exp(score_after - highest)
    weight_global = jnp.exp(score_global - highest)
    denominator = (
        jnp.sum(weight_before, axis=-1)
        + jnp.sum(weight_middle, axis=-1)
        + jnp.sum(weight_after, axis=-1)
        + jnp.sum(weight_global, axis=-1)
    )

    def local_values(weights, value_part):
        return jnp.einsum(
            "nqhk,nkhd->nqhd",
            weights.astype(jnp.bfloat16),
            value_part,
            preferred_element_type=jnp.float32,
        )

    summed = local_values(weight_before, value_before) + local_values(weight_middle, value_middle)
    summed = summed + local_values(weight_after, value_after)
    summed = summed + jnp.einsum(
        "nqhc,chd->nqhd",
        weight_global.astype(jnp.bfloat16),
        cov_values,
        preferred_element_type=jnp.float32,
    )
    result = (summed / denominator[..., None]).astype(jnp.bfloat16)
    return result.reshape(blocks * block_rows, attn_width)


def local(tokens, qkv_weight, cov_embed, cov_slot, block_links):
    tok_rows = tokens.shape[0]
    attn_width = qkv_weight.shape[1] // 3
    block_rows = BLOCK
    blocks = tok_rows // block_rows
    projected = jnp.dot(tokens, qkv_weight, preferred_element_type=jnp.float32).astype(jnp.bfloat16)
    queries = projected[:, :attn_width]
    keyvalue = projected[:, attn_width:]
    padded = extended(keyvalue, ((("grp", "seq"), 0),), block_rows)
    value_weight = qkv_weight[:, attn_width:]
    every_row = lax.all_gather(cov_embed, ("grp", "seq"), axis=0, tiled=True)
    chosen = jnp.take(every_row, cov_slot, axis=0)
    cov_kv = jnp.dot(chosen, value_weight, preferred_element_type=jnp.float32).astype(jnp.bfloat16)
    before = padded[:tok_rows].reshape(blocks, block_rows, 2 * attn_width)
    middle = keyvalue.reshape(blocks, block_rows, 2 * attn_width)
    after = padded[2 * block_rows : 2 * block_rows + tok_rows].reshape(
        blocks, block_rows, 2 * attn_width
    )
    return window_attend(
        queries.reshape(blocks, block_rows, attn_width),
        before,
        middle,
        after,
        block_links[:, 0],
        block_links[:, 1],
        cov_kv,
        HEADS,
    )


def solution(mesh):
    placed = (P(("grp", "seq"), None), P(), P(("grp", "seq"), None), P(), P(("grp", "seq"), None))
    return jax.shard_map(
        local, mesh=mesh, in_specs=placed, out_specs=P(("grp", "seq"), None), check_vma=False
    )
```

profile of v0, /device:TPU:0, one launch (start us, length us, event | category | flops | bytes accessed | tf_op | source)
XLA Modules:
  0.0 99.4 jit_solution(9266033365159456441)
XLA Ops:
  0.0 1.2 %copy-done = bf16[512,1024]{1,0:T(8,128)(2,1)S(1)} copy-done((bf16[512,1024]{1,0:T(8,128)(2,1)S(1)}, bf16[512,1024]{1,0:T(8,128)(2,1)}, u32[]{:S(2)}) %copy-start) | copy-done | bytes 1048600
  1.2 3.7 %convolution_convert_fusion = bf16[512,1536]{1,0:T(8,128)(2,1)S(1)} fusion(bf16[512,1024]{1,0:T(8,128)(2,1)S(1)} %copy-done, bf16[1024,1536]{1,0:T(8,128)(2,1)} %param.6), kind=kOutput, calls=%fused_computation.1 | convolution fusion | flops 1611399168 | bytes 5767168 | tf_op jit(solution)/shard_map/dot_general | solution.py:113
  5.8 2.4 %collective-permute-start = (bf16[128,1024]{1,0:T(8,128)(2,1)}, bf16[128,1024]{1,0:T(8,128)(2,1)S(1)}, u32[]{:S(2)}, u32[]{:S(2)}) collective-permute-start(bf16[128,1024]{1,0:T(8,128)(2,1)} %get-tuple-element.8), channel_id=1, source_target_pairs={{0,1},{1,2},{2,3},{3,4},{4,5},{5,6},{6,7},{7,8},{8,9},{9,10},{10,1... | collective-permute-start | bytes 786440 | tf_op jit(solution)/shard_map/ppermute | solution.py:23
  8.1 1.3 %collective-permute-start.1 = (bf16[128,1024]{1,0:T(8,128)(2,1)}, bf16[128,1024]{1,0:T(8,128)(2,1)}, u32[]{:S(2)}, u32[]{:S(2)}) collective-permute-start(bf16[128,1024]{1,0:T(8,128)(2,1)} %get-tuple-element.9), channel_id=1, source_target_pairs={{1,0},{2,1},{3,2},{4,3},{5,4},{6,5},{7,6},{8,7},{9,8},{10,9},{11,1... | collective-permute-start | bytes 786440 | tf_op jit(solution)/shard_map/ppermute | solution.py:25
  9.9 0.9 reshape_reshape.3
  10.8 0.9 fusion.58
  11.7 1.0 %copy.68 = bf16[4,128,512]{1,2,0:T(8,128)(2,1)} copy(bf16[4,128,512]{2,1,0:T(8,128)(2,1)S(1)} %get-tuple-element.13) | data formatting | bytes 1048576 | tf_op jit(solution)/shard_map/slice | solution.py:39
  12.7 45.4 %all-gather = bf16[32,2,1024]{2,1,0:T(2,128)(2,1)S(1)} all-gather(bf16[1,2,1024]{2,1,0:T(2,128)(2,1)S(1)} %bitcast.82), channel_id=1, replica_groups=mesh['grp'=2,'seq'=16] {'grp','seq'}, dimensions={0}, use_global_device_ids=true | all-gather | bytes 135168 | tf_op jit(solution)/shard_map/all_gather | solution.py:118
  58.9 2.2 %fusion.16 = bf16[32,1024]{1,0:T(8,128)(2,1)S(1)} fusion(bf16[1024,1536]{1,0:T(8,128)(2,1)} %param.6, bf16[32,1024]{1,0:T(8,128)(2,1)S(1)} %gather_fusion, pred[32]{0:T(512)(128)(4,1)S(1)} %compare_and_fusion), kind=kOutput, calls=%fused_computation.30 | convolution fusion | flops 67174400 | bytes 2228256 | tf_op jit(solution)/shard_map/dot_general | solution.py:120
  61.7 1.6 %bitcast_reduce_fusion.1 = (f32[4,128,8]{1,2,0:T(8,128)S(1)}, f32[4,8,128,128]{3,2,1,0:T(8,128)S(1)}) fusion(bf16[4,128,8,64]{1,3,2,0:T(8,128)(2,1)S(1)} %bitcast.76, bf16[4,128,8,64]{1,0,3,2:T(4,128)(2,1)} %reshape_reshape.3), kind=kOutput, calls=%fused_computation.6 | convolution fusion | flops 68153344 | bytes 3162112 | tf_op jit(solution)/shard_map/nqhd,nkhd->nqhk/dot_general | solution.py:52
  63.9 2.0 %copy.76 = bf16[4,128,512]{1,2,0:T(8,128)(2,1)} copy(bf16[4,128,512]{2,1,0:T(8,128)(2,1)} %get-tuple-element.12) | data formatting | bytes 1048576 | tf_op jit(solution)/shard_map/slice | solution.py:40
  66.8 2.7 %fusion.61 = (f32[4,128,8]{1,0,2:T(4,128)}, f32[4,128,8,32]{1,3,0,2:T(8,128)}) fusion(bf16[4,128,8,64]{1,0,3,2:T(4,128)(2,1)} %reshape_reshape.3, bf16[32,8,64,1]{2,1,0,3:T(8,128)(2,1)S(1)} %bitcast.81), kind=kOutput, calls=%fused_computation.80 | convolution fusion | flops 17035264 | bytes 1097728 | tf_op jit(solution)/shard_map/nqhd,chd->nqhc/dot_general | solution.py:64
  69.5 2.6 %pad_maximum_fusion.1 = (bf16[512,1024]{1,0:T(8,128)(2,1)S(1)}, bf16[512,1024]{1,0:T(8,128)(2,1)}) fusion(bf16[512,1024]{1,0:T(8,128)(2,1)} %copy-done.3, bf16[128,1024]{1,0:T(8,128)(2,1)S(1)} %collective-permute-done, bf16[128,1024]{1,0:T(8,128)(2,1)} %collective-permute-done.1), kind=kLoop, calls=%fused_computation.33 | loop fusion | flops 4194304 | bytes 3670016 | tf_op jit(solution)/shard_map/concatenate | solution.py:21
  72.1 1.1 %fusion.59 = (bf16[4,128,512]{2,1,0:T(8,128)(2,1)}, bf16[4,128,512]{2,1,0:T(8,128)(2,1)}) fusion(bf16[4,128,1024]{2,1,0:T(8,128)(2,1)S(1)} %bitcast.74), kind=kLoop, calls=%fused_computation.78 | loop fusion | bytes 2097152 | tf_op jit(solution)/shard_map/slice | solution.py:40
  73.2 2.0 %copy.65 = bf16[4,128,512]{1,2,0:T(8,128)(2,1)} copy(bf16[4,128,512]{2,1,0:T(8,128)(2,1)} %get-tuple-element.15) | data formatting | bytes 1048576 | tf_op jit(solution)/shard_map/slice | solution.py:39
  75.3 2.3 %fusion.57 = (bf16[4,128,512]{2,1,0:T(8,128)(2,1)}, bf16[4,128,512]{2,1,0:T(8,128)(2,1)}) fusion(bf16[4,128,1024]{2,1,0:T(8,128)(2,1)} %bitcast.73), kind=kLoop, calls=%fused_computation.76 | loop fusion | bytes 2097152 | tf_op jit(solution)/shard_map/slice | solution.py:40
  77.5 2.1 %copy.70 = bf16[4,128,512]{1,2,0:T(8,128)(2,1)} copy(bf16[4,128,512]{2,1,0:T(8,128)(2,1)} %get-tuple-element.11) | data formatting | bytes 1048576 | tf_op jit(solution)/shard_map/slice | solution.py:39
  79.6 3.3 %bitcast_reduce_fusion.2 = (f32[4,128,8]{1,2,0:T(8,128)S(1)}, f32[4,8,128,128]{3,2,1,0:T(8,128)}) fusion(pred[4]{0:T(512)(128)(4,1)S(1)} %copy-done.11, bf16[4,128,8,64]{1,3,2,0:T(8,128)(2,1)} %bitcast.77, bf16[4,128,8,64]{1,0,3,2:T(4,128)(2,1)} %reshape_reshape.3), kind=kOutput, calls=%fused_computation.9 | convolution fusion | flops 68677632 | bytes 3162116 | tf_op jit(solution)/shard_map/nqhd,nkhd->nqhk/dot_general | solution.py:52
  82.9 2.0 %bitcast_reduce_fusion = (f32[4,128,8]{1,2,0:T(8,128)S(1)}, f32[4,8,128,128]{3,2,1,0:T(8,128)}) fusion(pred[4]{0:T(512)(128)(4,1)S(1)} %copy-done.12, bf16[4,128,8,64]{1,3,2,0:T(8,128)(2,1)S(1)} %bitcast.78, bf16[4,128,8,64]{1,0,3,2:T(4,128)(2,1)S(1)} %copy-done.2), kind=kOutput, calls=%fused_computation.3 | convolution fusion | flops 68677632 | bytes 3162116 | tf_op jit(solution)/shard_map/nqhd,nkhd->nqhk/dot_general | solution.py:52
  84.9 2.0 %copy.64 = bf16[4,128,512]{1,2,0:T(8,128)(2,1)} copy(bf16[4,128,512]{2,1,0:T(8,128)(2,1)} %get-tuple-element.14) | data formatting | bytes 1048576 | tf_op jit(solution)/shard_map/slice | solution.py:40
  86.9 2.1 %copy.78 = bf16[4,128,512]{1,2,0:T(8,128)(2,1)} copy(bf16[4,128,512]{2,1,0:T(8,128)(2,1)} %get-tuple-element.10) | data formatting | bytes 1048576 | tf_op jit(solution)/shard_map/slice | solution.py:40
  89.0 2.6 %fusion.20 = f32[4,8,64,128]{3,2,1,0:T(8,128)S(1)} fusion(bf16[4,128,8,64]{1,3,2,0:T(8,128)(2,1)} %bitcast.79, f32[4,8,128,128]{3,2,1,0:T(8,128)} %get-tuple-element.29, f32[4,128,8]{1,2,0:T(8,128)S(1)} %fusion.49, pred[4]{0:T(512)(128)(4,1)S(1)} %copy-done.11), kind=kOutput, calls=%fused_computation.31 | convolution fusion | flops 69206016 | bytes 3686404 | tf_op jit(solution)/shard_map/nqhk,nkhd->nqhd/dot_general | solution.py:89
  91.6 3.2 %fusion.5 = (f32[4,128,8]{1,2,0:T(8,128)S(1)}, f32[4,128,8]{1,2,0:T(8,128)S(1)}, f32[4,128,8]{1,2,0:T(8,128)S(1)}) fusion(f32[4,8,128,128]{3,2,1,0:T(8,128)S(1)} %get-tuple-element.31, f32[4,128,8]{1,2,0:T(8,128)S(1)} %fusion.49, f32[4,8,128,128]{3,2,1,0:T(8,128)S(1)} %copy-done.1, pred[4]{0:T(512)(128)(4,1)S(1)} %copy-done.11, ...), kind=kLoop, calls=%fused_computation.15 | loop fusion | flops 5754880 | bytes 6357000 | tf_op jit(solution)/shard_map/reduce_sum | solution.py:83
  98.0 1.4 %reshape.105 = bf16[512,512]{1,0:T(8,128)(2,1)} reshape(bf16[4,128,8,64]{3,2,1,0:T(8,128)(2,1)S(1)} %copy.92) | data formatting | bytes 1048576 | tf_op jit(solution)/shard_map/reshape | solution.py:105
  (54 shorter events, 7.3 us)
Async XLA Ops:
  0.0 1.2 %copy-start = (bf16[512,1024]{1,0:T(8,128)(2,1)S(1)}, bf16[512,1024]{1,0:T(8,128)(2,1)}, u32[]{:S(2)}) copy-start(bf16[512,1024]{1,0:T(8,128)(2,1)} %param.5) | copy-start | bytes 3145732
  4.9 4.7 %copy-start.15 = (s32[32]{0:T(128)S(1)}, s32[32]{0:T(128)}, u32[]{:S(2)}) copy-start(s32[32]{0:T(128)} %param.8) | copy-start | bytes 388
  5.8 63.7 %collective-permute-start = (bf16[128,1024]{1,0:T(8,128)(2,1)}, bf16[128,1024]{1,0:T(8,128)(2,1)S(1)}, u32[]{:S(2)}, u32[]{:S(2)}) collective-permute-start(bf16[128,1024]{1,0:T(8,128)(2,1)} %get-tuple-element.8), channel_id=1, source_target_pairs={{0,1},{1,2},{2,3},{3,4},{4,5},{5,6},{6,7},{7,8},{8,9},{9,10},{10,1... | collective-permute-start | bytes 786440 | tf_op jit(solution)/shard_map/ppermute | solution.py:23
  8.1 61.4 %collective-permute-start.1 = (bf16[128,1024]{1,0:T(8,128)(2,1)}, bf16[128,1024]{1,0:T(8,128)(2,1)}, u32[]{:S(2)}, u32[]{:S(2)}) collective-permute-start(bf16[128,1024]{1,0:T(8,128)(2,1)} %get-tuple-element.9), channel_id=1, source_target_pairs={{1,0},{2,1},{3,2},{4,3},{5,4},{6,5},{7,6},{8,7},{9,8},{10,9},{11,1... | collective-permute-start | bytes 786440 | tf_op jit(solution)/shard_map/ppermute | solution.py:25
  9.6 2.2 %copy-start.3 = (bf16[512,1024]{1,0:T(8,128)(2,1)}, bf16[512,1024]{1,0:T(8,128)(2,1)S(1)}, u32[]{:S(2)}) copy-start(bf16[512,1024]{1,0:T(8,128)(2,1)S(1)} %slice.75) | copy-start | bytes 3145732
  9.9 2.8 %copy-start.13 = (bf16[2,1024]{1,0:T(2,128)(2,1)S(1)}, bf16[2,1024]{1,0:T(2,128)(2,1)}, u32[]{:S(2)}) copy-start(bf16[2,1024]{1,0:T(2,128)(2,1)} %param.7) | copy-start | bytes 12292
  58.9 2.8 %copy-start.7 = (bf16[4,128,512]{1,2,0:T(8,128)(2,1)S(1)}, bf16[4,128,512]{1,2,0:T(8,128)(2,1)}, u32[]{:S(2)}) copy-start(bf16[4,128,512]{1,2,0:T(8,128)(2,1)} %copy.68) | copy-start | bytes 1572868
  61.1 2.2 %copy-start.14 = (s32[4,2]{0,1:T(2,128)S(1)}, s32[4,2]{0,1:T(2,128)}, u32[]{:S(2)}) copy-start(s32[4,2]{0,1:T(2,128)} %param.9) | copy-start | bytes 100
  73.2 6.4 %copy-start.11 = (pred[4]{0:T(512)(128)(4,1)S(1)}, pred[4]{0:T(512)(128)(4,1)}, u32[]{:S(2)}) copy-start(pred[4]{0:T(512)(128)(4,1)} %get-tuple-element.22) | copy-start | bytes 16
  77.5 5.3 %copy-start.12 = (pred[4]{0:T(512)(128)(4,1)S(1)}, pred[4]{0:T(512)(128)(4,1)}, u32[]{:S(2)}) copy-start(pred[4]{0:T(512)(128)(4,1)} %get-tuple-element.23) | copy-start | bytes 16
  79.6 3.3 %copy-start.2 = (bf16[4,128,8,64]{1,0,3,2:T(4,128)(2,1)S(1)}, bf16[4,128,8,64]{1,0,3,2:T(4,128)(2,1)}, u32[]{:S(2)}) copy-start(bf16[4,128,8,64]{1,0,3,2:T(4,128)(2,1)} %reshape_reshape.3) | copy-start | bytes 1572868
  79.6 3.3 %copy-start.8 = (bf16[4,128,512]{1,2,0:T(8,128)(2,1)S(1)}, bf16[4,128,512]{1,2,0:T(8,128)(2,1)}, u32[]{:S(2)}) copy-start(bf16[4,128,512]{1,2,0:T(8,128)(2,1)} %copy.70) | copy-start | bytes 1572868
  82.9 2.0 %copy-start.10 = (f32[4,128,8]{1,0,2:T(4,128)S(1)}, f32[4,128,8]{1,0,2:T(4,128)}, u32[]{:S(2)}) copy-start(f32[4,128,8]{1,0,2:T(4,128)} %get-tuple-element.26) | copy-start | bytes 49156
  89.0 2.6 %copy-start.1 = (f32[4,8,128,128]{3,2,1,0:T(8,128)S(1)}, f32[4,8,128,128]{3,2,1,0:T(8,128)}, u32[]{:S(2)}) copy-start(f32[4,8,128,128]{3,2,1,0:T(8,128)} %get-tuple-element.29) | copy-start | bytes 6291460
  91.6 3.2 %copy-start.6 = (f32[4,128,8,32]{1,3,0,2:T(8,128)S(1)}, f32[4,128,8,32]{1,3,0,2:T(8,128)}, u32[]{:S(2)}) copy-start(f32[4,128,8,32]{1,3,0,2:T(8,128)} %get-tuple-element.27) | copy-start | bytes 1572868
  91.6 3.4 %copy-start.5 = (bf16[4,128,512]{1,2,0:T(8,128)(2,1)S(1)}, bf16[4,128,512]{1,2,0:T(8,128)(2,1)}, u32[]{:S(2)}) copy-start(bf16[4,128,512]{1,2,0:T(8,128)(2,1)} %copy.76) | copy-start | bytes 1572868
  95.0 1.6 %copy-start.4 = (f32[4,8,128,128]{3,2,1,0:T(8,128)S(1)}, f32[4,8,128,128]{3,2,1,0:T(8,128)}, u32[]{:S(2)}) copy-start(f32[4,8,128,128]{3,2,1,0:T(8,128)} %get-tuple-element.25) | copy-start | bytes 6291460
  95.0 1.7 %copy-start.9 = (bf16[4,128,512]{1,2,0:T(8,128)(2,1)S(1)}, bf16[4,128,512]{1,2,0:T(8,128)(2,1)}, u32[]{:S(2)}) copy-start(bf16[4,128,512]{1,2,0:T(8,128)(2,1)} %copy.78) | copy-start | bytes 1572868
where the time goes:
time: 100 us; the launch traced here: 99.4 us
  blocking collectives  45.4 us (45%)
  local copies, waits for them, and re-layouts  24 us (24%)
  matrix products  19.6 us (20%)
  other arithmetic  6.55 us (7%)
  starting transfers between devices  3.65 us (4%)
    all_gather x1, blocking collectives, local(): every_row = lax.all_gather(cov_embed, ('grp', 'seq'), axis=0, tiled=True)  45.4 us
    slice x6, local copies, waits for them, and re-layouts, divide_parts(): joined[:, :, attn_width:]  10.4 us
    dot_general x3, matrix products, local_scores(): jnp.einsum('nqhd,nkhd->nqhk', query_heads, key_part, preferred_element_ty...  6.79 us
    slice x3, local copies, waits for them, and re-layouts, divide_parts(): joined[:, :, :attn_width]  5.1 us
    dot_general x3, matrix products, local_values(): jnp.einsum('nqhk,nkhd->nqhd', weights.astype(jnp.bfloat16), value_part, p...  3.93 us
    dot_general x1, matrix products, local(): jnp.dot(tokens, qkv_weight, preferred_element_type=jnp.float32)  3.67 us
    reduce_sum x1, other arithmetic, window_attend(): jnp.sum(weight_middle, axis=-1)  3.2 us
    dot_general x1, matrix products, window_attend(): jnp.einsum('nqhd,chd->nqhc', query_heads, cov_keys, preferred_element_typ...  2.66 us
  transfers between devices with their start and end apart: 2, of which 0 were waited for; matrix products, arithmetic and copies ran while one was open for 15% of the time, Pallas kernels for 0%

commit v1 on v0

v1 whole, which is shorter than its diff:
```python
import functools
import math

import jax
import jax.numpy as jnp
from jax import lax
from jax.experimental import pallas as pl
from jax.experimental.pallas import tpu as pltpu
from jax.sharding import PartitionSpec as P

HEADS = 8
BLOCK = 128
LANES = 128
NT = (((1,), (1,)), ((), ()))
NN = (((1,), (0,)), ((), ()))
F32 = jnp.float32
BF16 = jnp.bfloat16
CLOSED = 1e30


def dot(a, b, dims=NN):
    return lax.dot_general(a, b, dims, preferred_element_type=F32)


def kernel(
    grid_shape,
    slot_ref,
    links_ref,
    x_hbm,
    w_hbm,
    cov_ref,
    out_ref,
    x,
    w,
    q,
    keys,
    values,
    cov_tmp,
    cov_mine,
    cov_all,
    cov_sum,
    load_sem,
    cov_send,
    cov_recv,
    halo_send,
    halo_recv,
):
    groups, seqs = grid_shape
    count = groups * seqs
    rows, depth = x.shape
    attn = q.shape[1]
    blocks = rows // BLOCK
    slots_dev = cov_ref.shape[0]
    pieces = depth // LANES
    tile_rows = slots_dev * pieces
    chosen_rows = slot_ref.shape[1]
    me = lax.axis_index("grp") * seqs + lax.axis_index("seq")

    def place(index):
        return (index // seqs, index % seqs)

    chunk = attn // 2
    order = [2, 3, 4, 5, 0, 1]
    loads = []
    x_load = pltpu.make_async_copy(x_hbm, x, load_sem.at[6])
    x_load.start()
    for i, c in enumerate(order):
        part = pl.ds(c * chunk, chunk)
        cp = pltpu.make_async_copy(w_hbm.at[:, part], w.at[:, part], load_sem.at[i])
        cp.start()
        loads.append(cp)

    barrier = pltpu.get_barrier_semaphore()

    @pl.loop(1, count)
    def _(step):
        pl.semaphore_signal(
            barrier,
            inc=1,
            device_id=place(lax.rem(me + step, count)),
            device_id_type=pl.DeviceIdType.MESH,
        )

    cov_value = cov_ref[...].astype(F32)
    for j in range(pieces):
        cov_tmp[j * slots_dev : (j + 1) * slots_dev, :] = cov_value[:, j * LANES : (j + 1) * LANES]
    cov_mine[...] = cov_tmp[...].astype(BF16)
    cov_all[me] = cov_mine[...]
    pl.semaphore_wait(barrier, count - 1)

    @pl.loop(1, count)
    def _(step):
        pltpu.make_async_remote_copy(
            src_ref=cov_mine,
            dst_ref=cov_all.at[me],
            send_sem=cov_send,
            recv_sem=cov_recv,
            device_id=place(lax.rem(me + step, count)),
            device_id_type=pl.DeviceIdType.MESH,
        ).start()

    x_load.wait()
    for i in range(4):
        loads[i].wait()
        c = order[i]
        part = dot(x[...], w[:, c * chunk : (c + 1) * chunk]).astype(BF16)
        if i < 2:
            keys[BLOCK : BLOCK + rows, i * chunk : (i + 1) * chunk] = part
        else:
            k = i - 2
            for b in range(blocks):
                values[b + 1, k * chunk : (k + 1) * chunk, :] = part[
                    b * BLOCK : (b + 1) * BLOCK, :
                ].T

    def key_rows(b):
        return keys.at[pl.ds(b * BLOCK, BLOCK)]

    def edge_copies(source, target, peer, at):
        return [
            pltpu.make_async_remote_copy(
                src_ref=src,
                dst_ref=dst,
                send_sem=halo_send.at[at + n],
                recv_sem=halo_recv.at[at + n],
                device_id=place(peer),
                device_id_type=pl.DeviceIdType.MESH,
            )
            for n, (src, dst) in enumerate(
                [
                    (key_rows(source), key_rows(target)),
                    (values.at[source], values.at[target]),
                ]
            )
        ]

    to_left = edge_copies(1, blocks + 1, lax.max(me - 1, 0), 0)
    to_right = edge_copies(blocks, 0, lax.min(me + 1, count - 1), 2)
    has_left = me > 0
    has_right = me < count - 1

    @pl.when(has_left)
    def _():
        for cp in to_left:
            cp.start()

    @pl.when(has_right)
    def _():
        for cp in to_right:
            cp.start()

    @pl.when(me == 0)
    def _():
        keys[0:BLOCK, :] = jnp.zeros((BLOCK, attn), BF16)
        values[0] = jnp.zeros((attn, BLOCK), BF16)

    @pl.when(me == count - 1)
    def _():
        keys[BLOCK + rows : 2 * BLOCK + rows, :] = jnp.zeros((BLOCK, attn), BF16)
        values[blocks + 1] = jnp.zeros((attn, BLOCK), BF16)

    for i in (4, 5):
        loads[i].wait()
        c = order[i]
        part = dot(x[...], w[:, c * chunk : (c + 1) * chunk]).astype(BF16)
        q[:, c * chunk : (c + 1) * chunk] = part

    others = cov_all.at[pl.ds(0, count - 1)]
    pltpu.make_async_copy(others, others, cov_recv).wait()
    span = 32 if count % 32 == 0 else count
    cov_sum[...] = jnp.zeros_like(cov_sum)

    @pl.loop(0, count // span)
    def _(t):
        held = cov_all[pl.ds(t * span, span)].reshape(span * tile_rows, LANES)
        slot = slot_ref[...]
        base = (slot // slots_dev - t * span) * tile_rows + slot % slots_dev
        row = lax.broadcasted_iota(jnp.int32, (span * tile_rows, chosen_rows), 0)
        for j in range(pieces):
            pick = jnp.where(row == base + j * slots_dev, 1.0, 0.0).astype(BF16)
            cov_sum[:, j * LANES : (j + 1) * LANES] += lax.dot_general(
                pick, held, (((0,), (0,)), ((), ())), preferred_element_type=F32
            )

    chosen = cov_sum[...].astype(BF16)
    cov_keys = dot(chosen, w[:, attn : 2 * attn]).astype(BF16)
    cov_values = dot(chosen, w[:, 2 * attn :]).astype(BF16).T

    factor = math.log2(math.e) / math.sqrt(attn // HEADS)
    lane = lax.broadcasted_iota(jnp.int32, (BLOCK, LANES), 1)
    low = lane < LANES // 2

    def attend(b, p):
        cols = slice(p * LANES, (p + 1) * LANES)
        qp = q[b * BLOCK : (b + 1) * BLOCK, cols]
        zero = jnp.zeros_like(qp)
        both = jnp.concatenate([jnp.where(low, qp, zero), jnp.where(low, zero, qp)], axis=0)
        scores = dot(keys[b * BLOCK : (b + 3) * BLOCK, cols], both, NT)
        score_cov = dot(cov_keys[:, cols], both, NT)
        before, middle, after = (scores[i * BLOCK : (i + 1) * BLOCK] for i in range(3))
        open_before = links_ref[b, 0] > 0
        open_after = links_ref[b, 1] > 0

        def top(s):
            return jnp.max(s, axis=0, keepdims=True)

        highest = jnp.maximum(
            jnp.maximum(top(middle), top(score_cov)),
            jnp.maximum(
                jnp.where(open_before, top(before), -CLOSED),
                jnp.where(open_after, top(after), -CLOSED),
            ),
        )
        weights = [
            jnp.exp2((before - jnp.where(open_before, highest, CLOSED)) * factor),
            jnp.exp2((middle - highest) * factor),
            jnp.exp2((after - jnp.where(open_after, highest, CLOSED)) * factor),
            jnp.exp2((score_cov - highest) * factor),
        ]
        total = sum(jnp.sum(a, axis=0, keepdims=True) for a in weights)
        rounded = jnp.concatenate([a.astype(BF16) for a in weights], axis=0)
        value = jnp.concatenate(
            [values[b, cols], values[b + 1, cols], values[b + 2, cols], cov_values[cols, :]],
            axis=1,
        )
        summed = dot(value, rounded) * (1.0 / total)
        half = LANES // 2
        pair = jnp.concatenate([summed[:half, :BLOCK], summed[half:, BLOCK:]], axis=0)
        out_ref[b * BLOCK : (b + 1) * BLOCK, cols] = pair.T.astype(BF16)

    for b in range(1, blocks - 1):
        for p in range(attn // LANES):
            attend(b, p)

    @pl.when(has_left)
    def _():
        for cp in to_right:
            cp.wait_recv()

    @pl.when(has_right)
    def _():
        for cp in to_left:
            cp.wait_recv()

    for b in (0, blocks - 1):
        for p in range(attn // LANES):
            attend(b, p)

    @pl.when(has_left)
    def _():
        for cp in to_left:
            cp.wait_send()

    @pl.when(has_right)
    def _():
        for cp in to_right:
            cp.wait_send()

    pltpu.make_async_copy(others, others, cov_send).wait()


def local(grid_shape, tokens, qkv_weight, cov_embed, cov_slot, block_links):
    count = grid_shape[0] * grid_shape[1]
    rows, depth = tokens.shape
    attn = qkv_weight.shape[1] // 3
    blocks = rows // BLOCK
    tile_rows = cov_embed.shape[0] * depth // LANES
    cov = cov_slot.shape[0]
    vmem = pl.BlockSpec(memory_space=pltpu.VMEM)
    smem = pl.BlockSpec(memory_space=pltpu.SMEM)
    hbm = pl.BlockSpec(memory_space=pl.ANY)
    return pl.pallas_call(
        functools.partial(kernel, grid_shape),
        out_shape=jax.ShapeDtypeStruct((rows, attn), BF16),
        in_specs=[vmem, smem, hbm, hbm, vmem],
        out_specs=vmem,
        scratch_shapes=[
            pltpu.VMEM((rows, depth), BF16),
            pltpu.VMEM((depth, 3 * attn), BF16),
            pltpu.VMEM((rows, attn), BF16),
            pltpu.VMEM((rows + 2 * BLOCK, attn), BF16),
            pltpu.VMEM((blocks + 2, attn, BLOCK), BF16),
            pltpu.VMEM((tile_rows, LANES), F32),
            pltpu.VMEM((tile_rows, LANES), BF16),
            pltpu.VMEM((count, tile_rows, LANES), BF16),
            pltpu.VMEM((cov, depth), F32),
            pltpu.SemaphoreType.DMA((7,)),
            pltpu.SemaphoreType.DMA,
            pltpu.SemaphoreType.DMA,
            pltpu.SemaphoreType.DMA((4,)),
            pltpu.SemaphoreType.DMA((4,)),
        ],
        compiler_params=pltpu.CompilerParams(
            collective_id=0, has_side_effects=True, vmem_limit_bytes=56 * 1024 * 1024
        ),
        cost_estimate=pl.CostEstimate(
            flops=2 * rows * depth * 3 * attn, bytes_accessed=5 << 20, transcendentals=rows * 4096
        ),
    )(cov_slot.reshape(1, cov), block_links, tokens, qkv_weight, cov_embed)


def solution(mesh):
    placed = (P(("grp", "seq"), None), P(), P(("grp", "seq"), None), P(), P(("grp", "seq"), None))
    grid_shape = (mesh.shape["grp"], mesh.shape["seq"])
    return jax.shard_map(
        functools.partial(local, grid_shape),
        mesh=mesh,
        in_specs=placed,
        out_specs=P(("grp", "seq"), None),
        check_vma=False,
    )
```

time: 100 us -> 23.4 us (0.23)
  the two profiles are of different devices: /device:TPU:0 before, /device:TPU:3 now
where the time goes in v1:
time: 23.4 us; the launch traced here: 23.2 us
  Pallas kernels  20 us (85%)
  local copies, waits for them, and re-layouts  3.2 us (14%)
    pallas_call x1, Pallas kernels, local(): pl.pallas_call(functools.partial(kernel, grid_shape), out_shape=jax.Shape...  20 us
    unnamed x2, local copies, waits for them, and re-layouts  3.2 us

profile of v1, /device:TPU:3, one launch (start us, length us, event | category | flops | bytes accessed | tf_op | source)
XLA Modules:
  0.0 23.2 jit_solution(6570733758224352107)
XLA Ops:
  0.0 1.3 %copy.6.links_ref = s32[4,2]{1,0:T(4,128)} copy(s32[4,2]{0,1:T(2,128)} %param.9) | data formatting | bytes 64 | tf_op args[4]
  1.3 20.0 %shard_map.55 = bf16[512,512]{1,0:T(8,128)(2,1)} custom-call(s32[1,32]{1,0:T(1,128)} %bitcast.1, s32[4,2]{1,0:T(4,128)} %copy.6.links_ref, bf16[512,1024]{1,0:T(8,128)(2,1)} %x_hbm.1, bf16[1024,1536]{1,0:T(8,128)(2,1)} %w_hbm.1, bf16[2,1024]{1,0:T(2,128)(2,1)} %cov_ref.1), custom_call_target="tpu_custom_call" | custom-call | flops 1610612736 | bytes 5242880 | tf_op jit(solution)/shard_map/pallas_call | solution.py:272
  21.3 1.9 %copy.8 = bf16[512,512]{1,0:T(8,128)(2,1)} copy(bf16[512,512]{1,0:T(8,128)(2,1)} %shard_map.55) | data formatting | bytes 1048576

commit v2 on v1

v2 whole, which is shorter than its diff:
```python
import functools
import math

import jax
import jax.numpy as jnp
from jax import lax
from jax.experimental import pallas as pl
from jax.experimental.pallas import tpu as pltpu
from jax.sharding import PartitionSpec as P

HEADS = 8
BLOCK = 128
LANES = 128
NT = (((1,), (1,)), ((), ()))
NN = (((1,), (0,)), ((), ()))
F32 = jnp.float32
BF16 = jnp.bfloat16
CLOSED = 1e30
INNER = 4


def dot(a, b, dims=NN):
    return lax.dot_general(a, b, dims, preferred_element_type=F32)


def kernel(
    grid_shape,
    slot_ref,
    links_ref,
    x_hbm,
    w_hbm,
    cov_ref,
    out_ref,
    x,
    w,
    q,
    keys,
    values,
    cov_tmp,
    cov_mine,
    cov_all,
    cov_sum,
    halo,
    load_sem,
    line_send,
    line_recv,
    plane_send,
    plane_recv,
    halo_send,
    halo_recv,
):
    groups, seqs = grid_shape
    count = groups * seqs
    rows, depth = x.shape
    attn = q.shape[1]
    blocks = rows // BLOCK
    slots_dev = cov_ref.shape[0]
    pieces = depth // LANES
    tile_rows = slots_dev * pieces
    chosen_rows = slot_ref.shape[1]
    me = lax.axis_index("grp") * seqs + lax.axis_index("seq")

    def place(index):
        return (index // seqs, index % seqs)

    inner = INNER if seqs % INNER == 0 else 1
    length = seqs // inner
    width = groups * inner
    seq = lax.axis_index("seq")
    at_line = seq // inner
    at_plane = lax.axis_index("grp") * inner + seq % inner

    def on_line(step):
        return (lax.axis_index("grp"), lax.rem(at_line + step, length) * inner + seq % inner)

    def on_plane(step):
        other = lax.rem(at_plane + step, width)
        return (other // inner, at_line * inner + other % inner)

    left = place(lax.max(me - 1, 0))
    right = place(lax.min(me + 1, count - 1))
    has_left = me > 0
    has_right = me < count - 1
    mesh_id = pl.DeviceIdType.MESH
    barrier = pltpu.get_barrier_semaphore()

    def greet(device):
        pl.semaphore_signal(barrier, inc=1, device_id=device, device_id_type=mesh_id)

    pl.when(has_left)(lambda: greet(left))
    pl.when(has_right)(lambda: greet(right))
    pl.loop(1, length)(lambda step: greet(on_line(step)))
    pl.loop(1, width)(lambda step: greet(on_plane(step)))

    loads = [pltpu.make_async_copy(x_hbm, x, load_sem.at[0])]
    parts = 4
    step_rows = depth // parts
    for i in range(parts):
        part = pl.ds(i * step_rows, step_rows)
        loads.append(pltpu.make_async_copy(w_hbm.at[part], w.at[part], load_sem.at[i + 1]))
    for cp in loads:
        cp.start()

    cov_value = cov_ref[...].astype(F32)
    for j in range(pieces):
        cov_tmp[j * slots_dev : (j + 1) * slots_dev, :] = cov_value[:, j * LANES : (j + 1) * LANES]
    cov_mine[...] = cov_tmp[...].astype(BF16)
    cov_all[at_plane, at_line] = cov_mine[...]

    @pl.when(me == 0)
    def _():
        halo[0] = jnp.zeros((BLOCK, depth), BF16)

    @pl.when(me == count - 1)
    def _():
        halo[1] = jnp.zeros((BLOCK, depth), BF16)

    pl.semaphore_wait(
        barrier, length + width - 2 + has_left.astype(jnp.int32) + has_right.astype(jnp.int32)
    )

    @pl.loop(1, length)
    def _(step):
        pltpu.make_async_remote_copy(
            src_ref=cov_mine,
            dst_ref=cov_all.at[at_plane, at_line],
            send_sem=line_send,
            recv_sem=line_recv,
            device_id=on_line(step),
            device_id_type=mesh_id,
        ).start()

    def edge(first, side, device):
        return pltpu.make_async_remote_copy(
            src_ref=x_hbm.at[pl.ds(first, BLOCK)],
            dst_ref=halo.at[side],
            send_sem=halo_send.at[side],
            recv_sem=halo_recv.at[side],
            device_id=device,
            device_id_type=mesh_id,
        )

    to_left = edge(0, 1, left)
    to_right = edge(rows - BLOCK, 0, right)
    pl.when(has_left)(to_left.start)
    pl.when(has_right)(to_right.start)

    if length > 1:
        others = cov_all.at[0, pl.ds(0, length - 1)]
        pltpu.make_async_copy(others, others, line_recv).wait()

    @pl.loop(1, width)
    def _(step):
        pltpu.make_async_remote_copy(
            src_ref=cov_all.at[at_plane],
            dst_ref=cov_all.at[at_plane],
            send_sem=plane_send,
            recv_sem=plane_recv,
            device_id=on_plane(step),
            device_id_type=mesh_id,
        ).start()

    for cp in loads:
        cp.wait()
    part = dot(x[...], w[:, attn:]).astype(BF16)
    keys[BLOCK : BLOCK + rows, :] = part[:, :attn]
    for b in range(blocks):
        values[b + 1] = part[b * BLOCK : (b + 1) * BLOCK, attn:].T
    q[...] = dot(x[...], w[:, :attn]).astype(BF16)

    planes = cov_all.at[pl.ds(0, width - 1)]
    pltpu.make_async_copy(planes, planes, plane_recv).wait()
    span = max(1, 32 // length)
    span = span if width % span == 0 else 1
    span_rows = span * length * tile_rows
    cov_sum[...] = jnp.zeros_like(cov_sum)

    @pl.loop(0, width // span)
    def _(t):
        held = cov_all[pl.ds(t * span, span)].reshape(span_rows, LANES)
        slot = slot_ref[...]
        device = slot // slots_dev
        where_seq = device % seqs
        plane = (device // seqs) * inner + where_seq % inner
        tile = (plane - t * span) * length + where_seq // inner
        base = tile * tile_rows + slot % slots_dev
        row = lax.broadcasted_iota(jnp.int32, (span_rows, chosen_rows), 0)
        for j in range(pieces):
            pick = jnp.where(row == base + j * slots_dev, 1.0, 0.0).astype(BF16)
            cov_sum[:, j * LANES : (j + 1) * LANES] += lax.dot_general(
                pick, held, (((0,), (0,)), ((), ())), preferred_element_type=F32
            )

    cov_kv = dot(cov_sum[...].astype(BF16), w[:, attn:]).astype(BF16)
    cov_keys = cov_kv[:, :attn]
    cov_values = cov_kv[:, attn:].T

    factor = math.log2(math.e) / math.sqrt(attn // HEADS)
    lane = lax.broadcasted_iota(jnp.int32, (BLOCK, LANES), 1)
    low = lane < LANES // 2

    def attend(b, p):
        cols = slice(p * LANES, (p + 1) * LANES)
        qp = q[b * BLOCK : (b + 1) * BLOCK, cols]
        zero = jnp.zeros_like(qp)
        both = jnp.concatenate([jnp.where(low, qp, zero), jnp.where(low, zero, qp)], axis=0)
        scores = dot(keys[b * BLOCK : (b + 3) * BLOCK, cols], both, NT)
        score_cov = dot(cov_keys[:, cols], both, NT)
        before, middle, after = (scores[i * BLOCK : (i + 1) * BLOCK] for i in range(3))
        open_before = links_ref[0, b] > 0
        open_after = links_ref[1, b] > 0

        def top(s):
            return jnp.max(s, axis=0, keepdims=True)

        highest = jnp.maximum(
            jnp.maximum(top(middle), top(score_cov)),
            jnp.maximum(
                jnp.where(open_before, top(before), -CLOSED),
                jnp.where(open_after, top(after), -CLOSED),
            ),
        )
        weights = [
            jnp.exp2((before - jnp.where(open_before, highest, CLOSED)) * factor),
            jnp.exp2((middle - highest) * factor),
            jnp.exp2((after - jnp.where(open_after, highest, CLOSED)) * factor),
            jnp.exp2((score_cov - highest) * factor),
        ]
        total = sum(jnp.sum(a, axis=0, keepdims=True) for a in weights)
        rounded = jnp.concatenate([a.astype(BF16) for a in weights], axis=0)
        value = jnp.concatenate(
            [values[b, cols], values[b + 1, cols], values[b + 2, cols], cov_values[cols, :]],
            axis=1,
        )
        summed = dot(value, rounded) * (1.0 / total)
        half = LANES // 2
        pair = jnp.concatenate([summed[:half, :BLOCK], summed[half:, BLOCK:]], axis=0)
        out_ref[b * BLOCK : (b + 1) * BLOCK, cols] = pair.T.astype(BF16)

    for b in range(1, blocks - 1):
        for p in range(attn // LANES):
            attend(b, p)

    pl.when(has_left)(to_right.wait_recv)
    pl.when(has_right)(to_left.wait_recv)
    part = dot(halo[...].reshape(2 * BLOCK, depth), w[:, attn:]).astype(BF16)
    keys[0:BLOCK, :] = part[:BLOCK, :attn]
    keys[BLOCK + rows : 2 * BLOCK + rows, :] = part[BLOCK:, :attn]
    values[0] = part[:BLOCK, attn:].T
    values[blocks + 1] = part[BLOCK:, attn:].T

    for b in (0, blocks - 1):
        for p in range(attn // LANES):
            attend(b, p)

    pl.when(has_left)(to_left.wait_send)
    pl.when(has_right)(to_right.wait_send)
    if length > 1:
        pltpu.make_async_copy(others, others, line_send).wait()
    pltpu.make_async_copy(planes, planes, plane_send).wait()


def local(grid_shape, tokens, qkv_weight, cov_embed, cov_slot, block_links):
    count = grid_shape[0] * grid_shape[1]
    rows, depth = tokens.shape
    attn = qkv_weight.shape[1] // 3
    blocks = rows // BLOCK
    tile_rows = cov_embed.shape[0] * depth // LANES
    cov = cov_slot.shape[0]
    width = grid_shape[0] * (INNER if grid_shape[1] % INNER == 0 else 1)
    vmem = pl.BlockSpec(memory_space=pltpu.VMEM)
    smem = pl.BlockSpec(memory_space=pltpu.SMEM)
    hbm = pl.BlockSpec(memory_space=pl.ANY)
    return pl.pallas_call(
        functools.partial(kernel, grid_shape),
        out_shape=pltpu.VMEM((rows, attn), BF16),
        in_specs=[vmem, smem, hbm, hbm, vmem],
        out_specs=vmem,
        scratch_shapes=[
            pltpu.VMEM((rows, depth), BF16),
            pltpu.VMEM((depth, 3 * attn), BF16),
            pltpu.VMEM((rows, attn), BF16),
            pltpu.VMEM((rows + 2 * BLOCK, attn), BF16),
            pltpu.VMEM((blocks + 2, attn, BLOCK), BF16),
            pltpu.VMEM((tile_rows, LANES), F32),
            pltpu.VMEM((tile_rows, LANES), BF16),
            pltpu.VMEM((width, count // width, tile_rows, LANES), BF16),
            pltpu.VMEM((cov, depth), F32),
            pltpu.VMEM((2, BLOCK, depth), BF16),
            pltpu.SemaphoreType.DMA((5,)),
            pltpu.SemaphoreType.DMA,
            pltpu.SemaphoreType.DMA,
            pltpu.SemaphoreType.DMA,
            pltpu.SemaphoreType.DMA,
            pltpu.SemaphoreType.DMA((2,)),
            pltpu.SemaphoreType.DMA((2,)),
        ],
        compiler_params=pltpu.CompilerParams(
            collective_id=0, has_side_effects=True, vmem_limit_bytes=56 * 1024 * 1024
        ),
        cost_estimate=pl.CostEstimate(
            flops=2 * rows * depth * 3 * attn, bytes_accessed=5 << 20, transcendentals=rows * 4096
        ),
    )(cov_slot.reshape(1, cov), block_links.T, tokens, qkv_weight, cov_embed)


def solution(mesh):
    placed = (P(("grp", "seq"), None), P(), P(("grp", "seq"), None), P(), P(("grp", "seq"), None))
    grid_shape = (mesh.shape["grp"], mesh.shape["seq"])
    return jax.shard_map(
        functools.partial(local, grid_shape),
        mesh=mesh,
        in_specs=placed,
        out_specs=P(("grp", "seq"), None),
        check_vma=False,
    )
```

time: 23.4 us -> 21.8 us (0.932)
  local copies, waits for them, and re-layouts: 3.2 us -> 0.8 us
  Pallas kernels: 20 us -> 20.9 us
    unnamed x2 -> x1, local copies, waits for them, and re-layouts: 3.2 us -> 0.8 us
    pallas_call x1, Pallas kernels: 20 us -> 20.9 us  [local(): pl.pallas_call(functools.partial(kernel, grid_shape), out_shape=pltpu.VME...]
where the time goes in v2:
time: 21.8 us; the launch traced here: 21.7 us
  Pallas kernels  20.9 us (96%)
  local copies, waits for them, and re-layouts  0.8 us (4%)
    pallas_call x1, Pallas kernels, local(): pl.pallas_call(functools.partial(kernel, grid_shape), out_shape=pltpu.VME...  20.9 us
    unnamed x1, local copies, waits for them, and re-layouts  0.8 us

profile of v2, /device:TPU:3, one launch (start us, length us, event | category | flops | bytes accessed | tf_op | source)
XLA Modules:
  0.0 21.7 jit_solution(15687948838605860860)
XLA Ops:
  0.0 20.9 %shard_map.55 = bf16[512,512]{1,0:T(8,128)(2,1)S(1)} custom-call(s32[1,32]{1,0:T(1,128)} %bitcast.3, s32[2,4]{1,0:T(2,128)} %bitcast.2, bf16[512,1024]{1,0:T(8,128)(2,1)} %x_hbm.1, bf16[1024,1536]{1,0:T(8,128)(2,1)} %w_hbm.1, bf16[2,1024]{1,0:T(2,128)(2,1)} %cov_ref.1), custom_call_target="tpu_custom_call" | custom-call | flops 1610612736 | bytes 5242880 | tf_op jit(solution)/shard_map/pallas_call | solution.py:274
  20.9 0.8 %copy.7 = bf16[512,512]{1,0:T(8,128)(2,1)} copy(bf16[512,512]{1,0:T(8,128)(2,1)S(1)} %shard_map.55) | data formatting | bytes 1048576

commit v3 on v1

--- a/solution.py
+++ b/solution.py
@@ -198,8 +198,8 @@
         scores = dot(keys[b * BLOCK : (b + 3) * BLOCK, cols], both, NT)
         score_cov = dot(cov_keys[:, cols], both, NT)
         before, middle, after = (scores[i * BLOCK : (i + 1) * BLOCK] for i in range(3))
-        open_before = links_ref[b, 0] > 0
-        open_after = links_ref[b, 1] > 0
+        open_before = links_ref[0, b] > 0
+        open_after = links_ref[1, b] > 0
 
         def top(s):
             return jnp.max(s, axis=0, keepdims=True)
@@ -271,7 +271,7 @@
     hbm = pl.BlockSpec(memory_space=pl.ANY)
     return pl.pallas_call(
         functools.partial(kernel, grid_shape),
-        out_shape=jax.ShapeDtypeStruct((rows, attn), BF16),
+        out_shape=pltpu.VMEM((rows, attn), BF16),
         in_specs=[vmem, smem, hbm, hbm, vmem],
         out_specs=vmem,
         scratch_shapes=[
@@ -296,7 +296,7 @@
         cost_estimate=pl.CostEstimate(
             flops=2 * rows * depth * 3 * attn, bytes_accessed=5 << 20, transcendentals=rows * 4096
         ),
-    )(cov_slot.reshape(1, cov), block_links, tokens, qkv_weight, cov_embed)
+    )(cov_slot.reshape(1, cov), block_links.T, tokens, qkv_weight, cov_embed)
 
 
 def solution(mesh):

time: 23.4 us -> 20.1 us (0.86)
  local copies, waits for them, and re-layouts: 3.2 us -> 0.8 us
  Pallas kernels: 20 us -> 19.2 us
    unnamed x2 -> x1, local copies, waits for them, and re-layouts: 3.2 us -> 0.8 us
    pallas_call x1, Pallas kernels: 20 us -> 19.2 us  [local(): pl.pallas_call(functools.partial(kernel, grid_shape), out_shape=pltpu.VME...]
where the time goes in v3:
time: 20.1 us; the launch traced here: 20 us
  Pallas kernels  19.2 us (96%)
  local copies, waits for them, and re-layouts  0.8 us (4%)
    pallas_call x1, Pallas kernels, local(): pl.pallas_call(functools.partial(kernel, grid_shape), out_shape=pltpu.VME...  19.2 us
    unnamed x1, local copies, waits for them, and re-layouts  0.8 us

profile of v3, /device:TPU:3, one launch (start us, length us, event | category | flops | bytes accessed | tf_op | source)
XLA Modules:
  0.0 20.0 jit_solution(13261153922428097358)
XLA Ops:
  0.0 19.2 %shard_map.55 = bf16[512,512]{1,0:T(8,128)(2,1)S(1)} custom-call(s32[1,32]{1,0:T(1,128)} %bitcast.3, s32[2,4]{1,0:T(2,128)} %bitcast.2, bf16[512,1024]{1,0:T(8,128)(2,1)} %x_hbm.1, bf16[1024,1536]{1,0:T(8,128)(2,1)} %w_hbm.1, bf16[2,1024]{1,0:T(2,128)(2,1)} %cov_ref.1), custom_call_target="tpu_custom_call" | custom-call | flops 1610612736 | bytes 5242880 | tf_op jit(solution)/shard_map/pallas_call | solution.py:272
  19.2 0.8 %copy.7 = bf16[512,512]{1,0:T(8,128)(2,1)} copy(bf16[512,512]{1,0:T(8,128)(2,1)S(1)} %shard_map.55) | data formatting | bytes 1048576

commit v4 on v3

--- a/solution.py
+++ b/solution.py
@@ -59,16 +59,14 @@
     def place(index):
         return (index // seqs, index % seqs)
 
-    chunk = attn // 2
-    order = [2, 3, 4, 5, 0, 1]
-    loads = []
-    x_load = pltpu.make_async_copy(x_hbm, x, load_sem.at[6])
-    x_load.start()
-    for i, c in enumerate(order):
-        part = pl.ds(c * chunk, chunk)
-        cp = pltpu.make_async_copy(w_hbm.at[:, part], w.at[:, part], load_sem.at[i])
+    loads = [pltpu.make_async_copy(x_hbm, x, load_sem.at[0])]
+    parts = 4
+    step_rows = depth // parts
+    for i in range(parts):
+        part = pl.ds(i * step_rows, step_rows)
+        loads.append(pltpu.make_async_copy(w_hbm.at[part], w.at[part], load_sem.at[i + 1]))
+    for cp in loads:
         cp.start()
-        loads.append(cp)
 
     barrier = pltpu.get_barrier_semaphore()
 
@@ -99,19 +97,12 @@
             device_id_type=pl.DeviceIdType.MESH,
         ).start()
 
-    x_load.wait()
-    for i in range(4):
-        loads[i].wait()
-        c = order[i]
-        part = dot(x[...], w[:, c * chunk : (c + 1) * chunk]).astype(BF16)
-        if i < 2:
-            keys[BLOCK : BLOCK + rows, i * chunk : (i + 1) * chunk] = part
-        else:
-            k = i - 2
-            for b in range(blocks):
-                values[b + 1, k * chunk : (k + 1) * chunk, :] = part[
-                    b * BLOCK : (b + 1) * BLOCK, :
-                ].T
+    for cp in loads:
+        cp.wait()
+    part = dot(x[...], w[:, attn:]).astype(BF16)
+    keys[BLOCK : BLOCK + rows, :] = part[:, :attn]
+    for b in range(blocks):
+        values[b + 1] = part[b * BLOCK : (b + 1) * BLOCK, attn:].T
 
     def key_rows(b):
         return keys.at[pl.ds(b * BLOCK, BLOCK)]
@@ -159,11 +150,7 @@
         keys[BLOCK + rows : 2 * BLOCK + rows, :] = jnp.zeros((BLOCK, attn), BF16)
         values[blocks + 1] = jnp.zeros((attn, BLOCK), BF16)
 
-    for i in (4, 5):
-        loads[i].wait()
-        c = order[i]
-        part = dot(x[...], w[:, c * chunk : (c + 1) * chunk]).astype(BF16)
-        q[:, c * chunk : (c + 1) * chunk] = part
+    q[...] = dot(x[...], w[:, :attn]).astype(BF16)
 
     others = cov_all.at[pl.ds(0, count - 1)]
     pltpu.make_async_copy(others, others, cov_recv).wait()

time: 20.1 us -> 21.2 us (1.055)
  the two profiles are of different devices: /device:TPU:3 before, /device:TPU:0 now
where the time goes in v4:
time: 21.2 us; the launch traced here: 21 us
  Pallas kernels  20.2 us (95%)
  local copies, waits for them, and re-layouts  0.8 us (4%)
    pallas_call x1, Pallas kernels, local(): pl.pallas_call(functools.partial(kernel, grid_shape), out_shape=pltpu.VME...  20.2 us
    unnamed x1, local copies, waits for them, and re-layouts  0.8 us

profile of v4, /device:TPU:0, one launch (start us, length us, event | category | flops | bytes accessed | tf_op | source)
XLA Modules:
  0.0 21.0 jit_solution(11022258560833360882)
XLA Ops:
  0.0 20.2 %shard_map.55 = bf16[512,512]{1,0:T(8,128)(2,1)S(1)} custom-call(s32[1,32]{1,0:T(1,128)} %bitcast.3, s32[2,4]{1,0:T(2,128)} %bitcast.2, bf16[512,1024]{1,0:T(8,128)(2,1)} %x_hbm.1, bf16[1024,1536]{1,0:T(8,128)(2,1)} %w_hbm.1, bf16[2,1024]{1,0:T(2,128)(2,1)} %cov_ref.1), custom_call_target="tpu_custom_call" | custom-call | flops 1610612736 | bytes 5242880 | tf_op jit(solution)/shard_map/pallas_call | solution.py:259
  20.2 0.8 %copy.7 = bf16[512,512]{1,0:T(8,128)(2,1)} copy(bf16[512,512]{1,0:T(8,128)(2,1)S(1)} %shard_map.55) | data formatting | bytes 1048576
